TPU v7x, 512 devices: a whole 4x4x16 slice. The times are simulated.
512 devices in a mesh: row: 16 (over z_lo, x), col: 32 (over y, z_hi, core).
Axes of the slice: x: 4, y: 4, z: 16 (z_hi: 4, z_lo: 4; z = z_hi * 4 + z_lo), core: 2. Of those that a mesh axis runs over, the one named last changes fastest.
Arguments:
- features: bfloat16 [131072, 128], P(('col', 'row')), may hold values from -6 to 6
- weight: bfloat16 [128, 128], replicated, may hold values from -0.5 to 0.5
- tile_values: bfloat16 [16, 32, 16, 128, 128], P('row', 'col'), may hold values from -0.1875 to 0.1875
- tile_rows: int32 [16, 32, 16], P('row', 'col'), may hold values from 0 to 63, as said below
- tile_cols: int32 [16, 32, 16], P('row', 'col'), may hold values from 0 to 31
- tile_count: int32 [16, 32], P('row', 'col'), may hold values from 4 to 16, as said below
- node_order: int32 [131072], P(('row', 'col')), may hold values from 0 to 131071, as said below
Outputs:
- activated: bfloat16 [131072, 128], P(('row', 'col'))
Inputs may be any that keep to these rules, and one draw needn't show every extreme that they name: `tile_count`: every grid cell uses at least 4 slots; in every grid row some cell uses all 16. `tile_rows`: within one grid cell, no two slots name tile rows of the same aligned block of 2 tile rows. `node_order`: A permutation that maps each aligned block of 256 nodes onto itself.
All inputs are finite; a program needn't handle non-finite values.
Results may differ from a plain program's by a relative error of at most 0.0049.
Values may be sent and summed in bfloat16 or wider, within the bound.
A program may use at most 64 MiB of HBM per device.

v0:
```python
import jax
import jax.numpy as jnp
from jax import lax
from jax.sharding import PartitionSpec as P


def on_device(features, weight, tile_values, tile_rows, tile_cols, tile_count, node_order):
    gathered = lax.all_gather(features, "row", axis=0, tiled=True)
    tile_size = tile_values.shape[-1]
    feature_width = features.shape[1]
    slot_count = tile_values.shape[2]
    local_rows = features.shape[0]
    local_tiles = local_rows // tile_size
    xtiles = gathered.reshape(-1, tile_size, feature_width)
    inputs = xtiles[tile_cols.reshape(-1)]
    tile_vals = tile_values.reshape(slot_count, tile_size, tile_size)
    products = jnp.einsum("ktu,kuf->ktf", tile_vals, inputs, preferred_element_type=jnp.float32)
    products = products.reshape(slot_count, tile_size * feature_width)
    active = jnp.arange(slot_count) < tile_count.reshape(())
    tile_row_ids = tile_rows.reshape(-1)
    whole_tiles = lax.axis_size("col") * local_tiles
    wanted = jnp.arange(whole_tiles)
    onehot = ((tile_row_ids[None, :] == wanted[:, None]) & active[None, :]).astype(jnp.float32)
    summed = jnp.dot(
        onehot, products, precision=lax.Precision.HIGHEST, preferred_element_type=jnp.float32
    )
    aggregated = lax.psum_scatter(
        summed.reshape(whole_tiles * tile_size, feature_width),
        "col",
        scatter_dimension=0,
        tiled=True,
    )
    aggregated_low = aggregated.astype(jnp.bfloat16)
    mixed = jnp.maximum(
        jnp.dot(aggregated_low, weight, preferred_element_type=jnp.float32), 0.0
    ).astype(jnp.bfloat16)
    return jnp.zeros_like(mixed).at[node_order % local_rows].set(mixed)


def solution(mesh):
    return jax.shard_map(
        on_device,
        mesh=mesh,
        in_specs=(
            P(("col", "row"), None),
            P(),
            P("row", "col", None, None, None),
            P("row", "col", None),
            P("row", "col", None),
            P("row", "col"),
            P(("row", "col")),
        ),
        out_specs=P(("row", "col"), None),
        check_vma=False,
    )
```

profile of v0, /device:TPU:1, one launch (start us, length us, event | category | flops | bytes accessed | tf_op | source)
XLA Modules:
  0.0 259.0 jit_solution(14236111971301853686)
XLA Ops:
  6.5 0.0 copy-start
  6.5 0.0 copy-start.3
  6.5 0.0 all-gather.2.cloned.1.call-start
  6.5 0.7 all-gather.2.cloned.1.call-update
  7.3 0.0 reduce-scatter.2.cloned.1.call-start
  8.0 0.7 fusion.13
  8.6 82.4 %all-gather.2.cloned.1.call-done = bf16[4096,128]{1,0:T(8,128)(2,1)} async-done(((bf16[256,128]{1,0:T(8,128)(2,1)}), bf16[4096,128]{1,0:T(8,128)(2,1)}) %all-gather.2.cloned.1.call-update) | async-done | bytes 1048592 | tf_op jit(solution)/shard_map/all_gather | solution.py:8
  91.1 1.9 gather_fusion
  92.9 0.0 copy-done
  93.0 0.5 convolution_bitcast_fusion
  93.5 0.3 copy.9
  93.8 0.0 copy-done.3
  93.8 4.0 %fusion.1 = f32[64,16384]{1,0:T(8,128)} fusion(f32[2,8,128,128]{3,2,1,0:T(8,128)S(1)} %bitcast.19, s32[16]{0:T(128)S(1)} %bitcast.21, pred[16]{0:T(512)(128)(4,1)S(1)} %iota_compare_fusion.1), kind=kOutput, calls=%fused_computation.5 | convolution fusion | flops 201328640 | bytes 5242960 | tf_op jit(solution)/shard_map/dot_general | solution.py:24
  97.9 4.9 %reshape.56 = f32[8192,128]{1,0:T(8,128)} reshape(f32[64,16384]{1,0:T(8,128)} %fusion.1) | data formatting | bytes 8388608 | tf_op jit(solution)/shard_map/reshape | solution.py:28
  102.7 0.0 copy-start.2
  102.7 0.0 copy-start.1
  102.7 0.0 reduce-scatter.2.cloned.1.call-update
  102.7 0.7 copy-done.2
  103.4 145.9 %reduce-scatter.2.cloned.1.call-done = f32[256,128]{1,0:T(8,128)} async-done(((f32[8192,128]{1,0:T(8,128)}), f32[256,128]{1,0:T(8,128)}) %reduce-scatter.2.cloned.1.call-update) | async-done | bytes 131088 | tf_op jit(solution)/shard_map/reduce_scatter | solution.py:27
  249.3 0.0 copy-done.1
  249.3 1.0 fusion
  250.4 1.8 scatter_custom_fusion
  (3 shorter events, 0.0 us)
Async XLA Ops:
  6.5 86.4 %copy-start = (bf16[1,1,16,128,128]{4,3,2,1,0:T(8,128)(2,1)S(1)}, bf16[1,1,16,128,128]{4,3,2,1,0:T(8,128)(2,1)}, u32[]{:S(2)}) copy-start(bf16[1,1,16,128,128]{4,3,2,1,0:T(8,128)(2,1)} %param.9) | copy-start | bytes 1572868
  6.5 87.3 %copy-start.3 = (s32[1,1,16]{2,1,0:T(1,128)S(1)}, s32[1,1,16]{2,1,0:T(1,128)}, u32[]{:S(2)}) copy-start(s32[1,1,16]{2,1,0:T(1,128)} %param.10) | copy-start | bytes 196
  6.5 84.5 %all-gather.2.cloned.1.call-start = ((), (), s32[]{:S(2)}) async-start(), calls=%async_computation.1 | async-start | bytes 1114112 | tf_op jit(solution)/shard_map/all_gather | solution.py:8
  7.3 242.0 %reduce-scatter.2.cloned.1.call-start = ((), (), s32[]{:S(2)}) async-start(), calls=%async_computation.2 | async-start | bytes 4325376 | tf_op jit(solution)/shard_map/reduce_scatter | solution.py:27
  102.7 0.7 copy-start.2
  102.7 146.6 %copy-start.1 = (bf16[128,128]{1,0:T(8,128)(2,1)S(1)}, bf16[128,128]{1,0:T(8,128)(2,1)}, u32[]{:S(2)}) copy-start(bf16[128,128]{1,0:T(8,128)(2,1)} %param.8) | copy-start | bytes 98308
Sparse Core Ops, SparseCore 0:
  9.4 81.5 all-gather.1
  102.9 146.3 reduce-scatter.1
where the time goes:
time: 259 us
  waiting for transfers between devices  229 us (88%)
  between operations  14.1 us (5%)
  local copies, waits for them, and re-layouts  9.49 us (4%)
  matrix products  5.59 us (2%)
    reduce_scatter x1, waiting for transfers between devices, on_device(): lax.psum_scatter(summed.reshape(whole_tiles * tile_size, feature_width),...  146 us
    all_gather x1, waiting for transfers between devices, on_device(): gathered = lax.all_gather(features, 'row', axis=0, tiled=True)  82.4 us
  transfers between devices with their start and end apart: 2, of which 2 were waited for; matrix products, arithmetic and copies ran while one was open for 0% of the time, Pallas kernels for 0%

commit v1 on v0

v1 whole, which is shorter than its diff:
```python
import functools

import jax
import jax.numpy as jnp
from jax import lax
from jax.experimental import pallas as pl
from jax.experimental.pallas import tpu as pltpu
from jax.sharding import PartitionSpec as P

MESH = pl.DeviceIdType.MESH
TILE = 128
SLOTS = 16
LINE = 4
FAR_FIRST = (2, 1, 3, 0)
RING = tuple((dy, dc) for dy in FAR_FIRST for dc in (1, 0))
OTHERS = RING[:-1]


def kernel(
    features,
    weight,
    tile_values,
    tile_rows,
    tile_cols,
    tile_count,
    node_order,
    out,
    gathered,
    tiles,
    products,
    flags_out,
    flags_in,
    ring_out,
    ring_in,
    sums_out,
    sums_in,
    tiles_sem,
    gather_send,
    gather_recv,
    flags_send,
    flags_recv,
    ring_send,
    ring_recv,
    sums_send,
    sums_recv,
):
    row, col = lax.axis_index("row"), lax.axis_index("col")
    z, x = row // LINE, row % LINE
    y, h, core = col // 8, (col // 2) % LINE, col % 2

    def in_row(z_at, x_at):
        return (z_at * LINE + x_at, col)

    def in_col(dy, dh, dc):
        return (row, ((y + dy) % LINE) * 8 + ((h + dh) % LINE) * 2 + (core + dc) % 2)

    def send(src, dst, send_sem, recv_sem, device):
        copy = pltpu.make_async_remote_copy(
            src_ref=src, dst_ref=dst, send_sem=send_sem, recv_sem=recv_sem, device_id=device, device_id_type=MESH
        )
        copy.start()
        return copy

    pending = []

    load_tiles = pltpu.make_async_copy(tile_values.at[0, 0], tiles, tiles_sem.at[0])
    load_tiles.start()
    load_mine = pltpu.make_async_copy(features, gathered.at[pl.ds(2 * row, 2)], tiles_sem.at[1])
    load_mine.start()

    barrier = pltpu.get_barrier_semaphore()
    partners = (
        [in_row((z + d) % LINE, x) for d in (1, 2, 3)]
        + [in_row(z, (x + d) % LINE) for d in (1, 2, 3)]
        + [in_col(dy, 0, dc) for dy, dc in OTHERS]
        + [in_col(0, dh, 0) for dh in (1, 2, 3)]
    )
    for device in partners:
        pl.semaphore_signal(barrier, inc=1, device_id=device, device_id_type=MESH)
    pl.semaphore_wait(barrier, len(partners))

    def block(z_at, x_at):
        return gathered.at[pl.ds(2 * (z_at * LINE + x_at), 2)]

    sends = 0
    for d in (1, 3, 2):
        pending.append(
            send(features, block(z, x), gather_send.at[sends], gather_recv.at[row], in_row((z + d) % LINE, x))
        )
        sends += 1
    for d in (2, 1, 3):
        pending.append(
            send(features, block(z, x), gather_send.at[sends], gather_recv.at[row], in_row(z, (x + d) % LINE))
        )
        sends += 1

    count = tile_count[0, 0]
    owners = [jnp.where(k < count, tile_rows[0, 0, k] // 2, -1) for k in range(SLOTS)]
    codes = [2 * k + tile_rows[0, 0, k] % 2 for k in range(SLOTS)]

    def code_of(dy, dh, dc):
        owner = in_col(dy, dh, dc)[1]
        code = 2 * SLOTS
        for k in range(SLOTS):
            code = jnp.where(owners[k] == owner, codes[k], code)
        return code

    code = {}
    for i, (dy, dc) in enumerate(RING):
        for dh in range(LINE):
            code[i, dh] = code_of(dy, dh, dc)
            flags_out[i, dh, :] = jnp.full((TILE,), code[i, dh] % 2, jnp.float32)
    for i, (dy, dc) in enumerate(OTHERS):
        pending.append(
            send(flags_out.at[i], flags_in.at[i], flags_send.at[i], flags_recv.at[i], in_col(dy, 0, dc))
        )

    near = [jnp.where(z % 2 == 0, z + 1, z - 1), jnp.where(z < 2, 2, 1), jnp.where(z < 2, 3, 0)]
    for z_from in near:
        held = block(z_from, x)
        slot = z_from * LINE + x
        pltpu.make_async_copy(held, held, gather_recv.at[slot]).wait()
        for d in (2, 1, 3):
            pending.append(
                send(held, held, gather_send.at[sends], gather_recv.at[slot], in_row(z, (x + d) % LINE))
            )
            sends += 1
    for z_from in [z] + near:
        for d in (1, 3, 2):
            x_from = (x + d) % LINE
            held = block(z_from, x_from)
            pltpu.make_async_copy(held, held, gather_recv.at[z_from * LINE + x_from]).wait()

    load_tiles.wait()
    load_mine.wait()
    products[SLOTS] = jnp.zeros((TILE, TILE), jnp.bfloat16)
    for k in range(SLOTS):
        inputs = gathered[tile_cols[0, 0, k]]
        products[k] = jnp.dot(tiles[k], inputs, preferred_element_type=jnp.float32).astype(jnp.bfloat16)

    for dh in FAR_FIRST:
        for i, (dy, dc) in enumerate(OTHERS):
            ring_out[dh, i] = products[code[i, dh] // 2]
            pending.append(
                send(ring_out.at[dh, i], ring_in.at[dh, i], ring_send.at[dh, i], ring_recv.at[dh, i], in_col(dy, 0, dc))
            )

    for i in range(len(OTHERS)):
        pltpu.make_async_copy(flags_in.at[i], flags_in.at[i], flags_recv.at[i]).wait()
    sums = None
    mine = len(OTHERS)
    for dh in FAR_FIRST:
        tile = products[code[mine, dh] // 2].astype(jnp.float32)
        second = flags_out[mine, dh, :][None, :] > 0.5
        sums = [jnp.where(second, 0.0, tile), jnp.where(second, tile, 0.0)]
        for i in range(len(OTHERS)):
            pltpu.make_async_copy(ring_in.at[dh, i], ring_in.at[dh, i], ring_recv.at[dh, i]).wait()
            tile = ring_in[dh, i].astype(jnp.float32)
            second = flags_in[i, dh, :][None, :] > 0.5
            sums = [sums[0] + jnp.where(second, 0.0, tile), sums[1] + jnp.where(second, tile, 0.0)]
        if dh:
            sums_out[dh - 1, 0] = sums[0].astype(jnp.bfloat16)
            sums_out[dh - 1, 1] = sums[1].astype(jnp.bfloat16)
            pending.append(
                send(
                    sums_out.at[dh - 1],
                    sums_in.at[dh - 1],
                    sums_send.at[dh - 1],
                    sums_recv.at[dh - 1],
                    in_col(0, dh, 0),
                )
            )

    for dh in (1, 3, 2):
        pltpu.make_async_copy(sums_in.at[dh - 1], sums_in.at[dh - 1], sums_recv.at[dh - 1]).wait()
        sums = [sums[s] + sums_in[dh - 1, s].astype(jnp.float32) for s in range(2)]
    low = jnp.concatenate(sums, axis=0).astype(jnp.bfloat16)
    mixed = jnp.maximum(jnp.dot(low, weight[...], preferred_element_type=jnp.float32), 0.0).astype(jnp.bfloat16)
    nodes = 2 * TILE
    place = (node_order[...] % nodes)[None, :]
    wanted = lax.broadcasted_iota(jnp.int32, (nodes, nodes), 0)
    moves = jnp.where(wanted == place, 1.0, 0.0).astype(jnp.bfloat16)
    out[...] = jnp.dot(moves, mixed, preferred_element_type=jnp.float32).astype(jnp.bfloat16)

    for copy in pending:
        copy.wait_send()


def on_device(features, weight, tile_values, tile_rows, tile_cols, tile_count, node_order):
    vmem = pl.BlockSpec(memory_space=pltpu.VMEM)
    smem = pl.BlockSpec(memory_space=pltpu.SMEM)
    hbm = pl.BlockSpec(memory_space=pl.ANY)
    dma = pltpu.SemaphoreType.DMA
    others = len(OTHERS)
    return pl.pallas_call(
        kernel,
        out_shape=jax.ShapeDtypeStruct(features.shape, features.dtype),
        in_specs=[hbm, vmem, hbm, smem, smem, smem, vmem],
        out_specs=vmem,
        scratch_shapes=[
            pltpu.VMEM((2 * LINE * LINE, TILE, TILE), jnp.bfloat16),
            pltpu.VMEM((SLOTS, TILE, TILE), jnp.bfloat16),
            pltpu.VMEM((SLOTS + 1, TILE, TILE), jnp.bfloat16),
            pltpu.VMEM((others + 1, 8, TILE), jnp.float32),
            pltpu.VMEM((others, 8, TILE), jnp.float32),
            pltpu.VMEM((LINE, others, TILE, TILE), jnp.bfloat16),
            pltpu.VMEM((LINE, others, TILE, TILE), jnp.bfloat16),
            pltpu.VMEM((LINE - 1, 2, TILE, TILE), jnp.bfloat16),
            pltpu.VMEM((LINE - 1, 2, TILE, TILE), jnp.bfloat16),
            dma((2,)),
            dma((15,)),
            dma((LINE * LINE,)),
            dma((others,)),
            dma((others,)),
            dma((LINE, others)),
            dma((LINE, others)),
            dma((LINE - 1,)),
            dma((LINE - 1,)),
        ],
        compiler_params=pltpu.CompilerParams(
            collective_id=0, has_side_effects=True, vmem_limit_bytes=32 * 2**20
        ),
        name="graph_convolution",
    )(features.reshape(2, TILE, TILE), weight, tile_values, tile_rows, tile_cols, tile_count, node_order)


def solution(mesh):
    return jax.shard_map(
        on_device,
        mesh=mesh,
        in_specs=(
            P(("col", "row"), None),
            P(),
            P("row", "col", None, None, None),
            P("row", "col", None),
            P("row", "col", None),
            P("row", "col"),
            P(("row", "col")),
        ),
        out_specs=P(("row", "col"), None),
        check_vma=False,
    )
```

time: 259 us -> 57.1 us (0.22)
  waiting for transfers between devices: 229 us -> 0 us
  Pallas kernels: 0 us -> 52.2 us
  between operations: 14.1 us -> 0.7 us
  matrix products: 5.59 us -> 0 us
  local copies, waits for them, and re-layouts: 9.49 us -> 3.93 us
    reduce_scatter x1 -> x0, waiting for transfers between devices: 146 us -> none  [on_device(): lax.psum_scatter(summed.reshape(whole_tiles * tile_size, feature_width),...]
    all_gather x1 -> x0, waiting for transfers between devices: 82.4 us -> none  [on_device(): gathered = lax.all_gather(features, 'row', axis=0, tiled=True)]
    pallas_call x0 -> x1, Pallas kernels: none -> 52.2 us  [on_device(): pl.pallas_call(kernel, out_shape=jax.ShapeDtypeStruct(features.shape, fea...]
    dot_general x3 -> x0, matrix products: 5.59 us -> none  [the longest x1 4.03 us: on_device(): jnp.dot(onehot, products, precision=lax.Precision.HIGHEST, preferred_elem...]
    reshape x1 -> x0, local copies, waits for them, and re-layouts: 4.87 us -> none  [on_device(): summed.reshape(whole_tiles * tile_size, feature_width)]
    unnamed x8 -> x13, local copies, waits for them, and re-layouts: 0.66 us -> 3.93 us
  transfers between devices with their start and end apart: 2 -> 0, of which waited for: 2 -> 0; matrix products, arithmetic and copies ran while one was open for 0% -> 0% of each run, Pallas kernels for 0% -> 0%
where the time goes in v1:
time: 57.1 us; the launch traced here: 56.8 us
  Pallas kernels  52.2 us (91%)
  local copies, waits for them, and re-layouts  3.93 us (7%)
  between operations  0.7 us (1%)
    pallas_call x1, Pallas kernels, on_device(): pl.pallas_call(kernel, out_shape=jax.ShapeDtypeStruct(features.shape, fea...  52.2 us
    unnamed x13, local copies, waits for them, and re-layouts  3.93 us

profile of v1, /device:TPU:1, one launch (start us, length us, event | category | flops | bytes accessed | tf_op | source)
XLA Modules:
  0.0 56.8 jit_solution(8713670570927068568)
XLA Ops:
  0.0 0.0 copy-start.5
  0.7 0.0 copy-start.3
  0.7 0.0 copy-start.4
  0.7 0.0 copy-done.5
  0.7 0.7 %copy-done.3 = s32[256]{0:T(256)S(1)} copy-done((s32[256]{0:T(256)S(1)}, s32[256]{0:T(256)}, u32[]{:S(2)}) %copy-start.3) | copy-done | bytes 1048
  1.3 0.0 copy-done.4
  1.4 0.0 copy-start
  1.4 1.0 %copy-done = bf16[1,1,16,128,128]{4,3,2,1,0:T(8,128)(2,1)S(1)} copy-done((bf16[1,1,16,128,128]{4,3,2,1,0:T(8,128)(2,1)S(1)}, bf16[1,1,16,128,128]{4,3,2,1,0:T(8,128)(2,1)}, u32[]{:S(2)}) %copy-start) | copy-done | bytes 524312
  2.4 0.0 copy-start.1
  2.4 0.8 %copy-done.1 = bf16[256,128]{1,0:T(8,128)(2,1)S(1)} copy-done((bf16[256,128]{1,0:T(8,128)(2,1)S(1)}, bf16[256,128]{1,0:T(8,128)(2,1)}, u32[]{:S(2)}) %copy-start.1) | copy-done | bytes 65560
  3.2 0.0 copy-start.2
  3.2 0.8 %copy-done.2 = bf16[128,128]{1,0:T(8,128)(2,1)S(1)} copy-done((bf16[128,128]{1,0:T(8,128)(2,1)S(1)}, bf16[128,128]{1,0:T(8,128)(2,1)}, u32[]{:S(2)}) %copy-start.2) | copy-done | bytes 32792
  4.0 52.2 %graph_convolution.1 = bf16[256,128]{1,0:T(8,128)(2,1)S(1)} custom-call(bf16[2,128,128]{2,1,0:T(8,128)(2,1)S(1)} %bitcast.1, bf16[128,128]{1,0:T(8,128)(2,1)S(1)} %copy-done.2, bf16[1,1,16,128,128]{4,3,2,1,0:T(8,128)(2,1)S(1)} %copy-done, s32[1,1,16]{2,1,0:T(1,128)S(1)} %copy-done.4, s32[1,1,16]{2,1,0:T(1,128)S(1)} %copy-done.5, s32[1,1]{1,0:T(1,128)S(6)} %copy.9.tile_count, ...), custom_call_target="tpu_custom_call" | custom-call | tf_op jit(solution)/shard_map/graph_convolution/pallas_call | solution.py:195
  56.2 0.6 %copy.10 = bf16[256,128]{1,0:T(8,128)(2,1)} copy(bf16[256,128]{1,0:T(8,128)(2,1)S(1)} %graph_convolution.1) | data formatting | bytes 131072
Async XLA Ops:
  0.0 0.7 %copy-start.5 = (s32[1,1,16]{2,1,0:T(1,128)S(1)}, s32[1,1,16]{2,1,0:T(1,128)}, u32[]{:S(2)}) copy-start(s32[1,1,16]{2,1,0:T(1,128)} %tile_cols.1) | copy-start | bytes 196
  0.7 0.7 %copy-start.3 = (s32[256]{0:T(256)S(1)}, s32[256]{0:T(256)}, u32[]{:S(2)}) copy-start(s32[256]{0:T(256)} %node_order.1) | copy-start | bytes 3076
  0.7 0.7 %copy-start.4 = (s32[1,1,16]{2,1,0:T(1,128)S(1)}, s32[1,1,16]{2,1,0:T(1,128)}, u32[]{:S(2)}) copy-start(s32[1,1,16]{2,1,0:T(1,128)} %tile_rows.1) | copy-start | bytes 196
  1.4 1.0 %copy-start = (bf16[1,1,16,128,128]{4,3,2,1,0:T(8,128)(2,1)S(1)}, bf16[1,1,16,128,128]{4,3,2,1,0:T(8,128)(2,1)}, u32[]{:S(2)}) copy-start(bf16[1,1,16,128,128]{4,3,2,1,0:T(8,128)(2,1)} %tile_values.1) | copy-start | bytes 1572868
  2.4 0.8 %copy-start.1 = (bf16[256,128]{1,0:T(8,128)(2,1)S(1)}, bf16[256,128]{1,0:T(8,128)(2,1)}, u32[]{:S(2)}) copy-start(bf16[256,128]{1,0:T(8,128)(2,1)} %param.7) | copy-start | bytes 196612
  3.2 0.8 %copy-start.2 = (bf16[128,128]{1,0:T(8,128)(2,1)S(1)}, bf16[128,128]{1,0:T(8,128)(2,1)}, u32[]{:S(2)}) copy-start(bf16[128,128]{1,0:T(8,128)(2,1)} %weight.1) | copy-start | bytes 98308

commit v2 on v0

v2 whole, which is shorter than its diff:
```python
import jax
import jax.numpy as jnp
from jax import lax
from jax.experimental import pallas as pl
from jax.experimental.pallas import tpu as pltpu
from jax.sharding import PartitionSpec as P

MESH = pl.DeviceIdType.MESH
TILE = 128
HALF = TILE // 2
SLOTS = 16
LINE = 4
CELLS = LINE * LINE
RING = tuple((dy, dc) for dy in (2, 1, 3, 0) for dc in (1, 0))
OTHERS = RING[:-1]
MINE = len(OTHERS)
WAYS = ((1, 3), (3, 1))
PAIRS = tuple(((2, way), (back, 0)) for way, back in WAYS)
FAR, SUM, DIRECT = range(3)


def kernel(
    features_hbm,
    weight_hbm,
    tile_values_hbm,
    tile_rows_hbm,
    tile_cols_hbm,
    tile_count_hbm,
    node_order_hbm,
    out,
    features,
    weight,
    tiles,
    tile_rows,
    tile_cols,
    tile_count,
    node_order,
    gathered_a,
    gathered_b,
    products,
    moves,
    flags_out,
    flags_in,
    ring_out,
    ring_in,
    sums_out,
    sums_in,
    load_sem,
    gather_send,
    gather_recv,
    flags_send,
    flags_recv,
    ring_send,
    ring_recv,
    sums_send,
    sums_recv,
):
    row, col = lax.axis_index("row"), lax.axis_index("col")
    z, x = row // LINE, row % LINE
    y, h, core = col // 8, (col // 2) % LINE, col % 2
    first_lanes = lax.broadcasted_iota(jnp.int32, (TILE, TILE), 1) < HALF

    def in_row(z_at, x_at):
        return (z_at * LINE + x_at, col)

    def in_col(dy, dh, dc):
        return (row, ((y + dy) % LINE) * 8 + ((h + dh) % LINE) * 2 + (core + dc) % 2)

    gathered = (gathered_a, gathered_b)
    pending = []

    def send(src, dst, send_sem, recv_sem, device):
        copy = pltpu.make_async_remote_copy(
            src_ref=src, dst_ref=dst, send_sem=send_sem, recv_sem=recv_sem, device_id=device, device_id_type=MESH
        )
        copy.start()
        pending.append(copy)

    def arrived(ref, sem):
        pltpu.make_async_copy(ref, ref, sem).wait()

    def swap(value):
        return pltpu.roll(value, HALF, 1)

    barrier = pltpu.get_barrier_semaphore()
    partners = (
        [in_row((z + d) % LINE, x) for d in (1, 2, 3)]
        + [in_row(z, (x + d) % LINE) for d in (1, 2, 3)]
        + [in_col(dy, 0, dc) for dy, dc in OTHERS]
        + [in_col(0, dh, 0) for dh in (1, 3)]
    )
    for device in partners:
        pl.semaphore_signal(barrier, inc=1, device_id=device, device_id_type=MESH)

    loads = [
        pltpu.make_async_copy(src, dst, load_sem.at[i])
        for i, (src, dst) in enumerate(
            (
                (features_hbm, features),
                (tile_rows_hbm, tile_rows),
                (tile_cols_hbm, tile_cols),
                (tile_count_hbm, tile_count),
                (tile_values_hbm.at[0, 0], tiles),
                (node_order_hbm, node_order),
                (weight_hbm, weight),
            )
        )
    ]
    for load in loads:
        load.start()

    loads[0].wait()
    near_tile, next_tile = features[0].astype(jnp.float32), features[1].astype(jnp.float32)
    gathered_a[row] = jnp.where(first_lanes, near_tile, swap(next_tile)).astype(jnp.bfloat16)
    gathered_b[row] = jnp.where(first_lanes, swap(near_tile), next_tile).astype(jnp.bfloat16)
    pl.semaphore_wait(barrier, len(partners))

    sends = [0]

    def send_block(half, slot, device):
        block = gathered[half].at[slot]
        send(block, block, gather_send.at[sends[0]], gather_recv.at[half, slot], device)
        sends[0] += 1

    def send_along_z(half):
        for d in (1, 3, 2):
            send_block(half, row, in_row((z + d) % LINE, x))

    def send_along_x(half, z_from):
        for d in (2, 1, 3):
            send_block(half, z_from * LINE + x, in_row(z, (x + d) % LINE))

    near = [jnp.where(z % 2 == 0, z + 1, z - 1), jnp.where(z < 2, 2, 1), jnp.where(z < 2, 3, 0)]

    def forward(half):
        for z_from in near:
            slot = z_from * LINE + x
            arrived(gathered[half].at[slot], gather_recv.at[half, slot])
            send_along_x(half, z_from)

    def gather_end(half):
        for z_from in [z] + near:
            for d in (1, 3, 2):
                slot = z_from * LINE + (x + d) % LINE
                arrived(gathered[half].at[slot], gather_recv.at[half, slot])

    send_along_z(0)
    send_along_x(0, z)
    send_along_z(1)

    for load in loads[1:4]:
        load.wait()
    count = tile_count[0, 0]
    owners = [jnp.where(k < count, tile_rows[0, 0, k] // 2, -1) for k in range(SLOTS)]
    codes = [2 * k + tile_rows[0, 0, k] % 2 for k in range(SLOTS)]

    def code_of(dy, dh, dc):
        owner = in_col(dy, dh, dc)[1]
        code = 2 * SLOTS
        for k in range(SLOTS):
            code = jnp.where(owners[k] == owner, codes[k], code)
        return code

    forward(0)
    send_along_x(1, z)

    code = {(i, dh): code_of(dy, dh, dc) for i, (dy, dc) in enumerate(RING) for dh in range(LINE)}
    lanes = lax.broadcasted_iota(jnp.int32, (1, TILE), 1) < HALF
    for i in range(len(RING)):
        for half in range(2):
            for pair, (one, two) in enumerate(PAIRS[half]):
                second = jnp.where(lanes, code[i, one] % 2, code[i, two] % 2).astype(jnp.float32)
                flags_out[i, pl.ds(2 * half + pair, 1), :] = second
    for i, (dy, dc) in enumerate(OTHERS):
        send(flags_out.at[i], flags_in.at[i], flags_send.at[i], flags_recv.at[i], in_col(dy, 0, dc))

    forward(1)

    for load in loads[4:]:
        load.wait()

    def multiply(half):
        products[half, SLOTS] = jnp.zeros((TILE, TILE), jnp.bfloat16)
        for k in range(SLOTS):
            from_tile = tile_cols[0, 0, k]
            both = jnp.dot(tiles[k], gathered[half][from_tile // 2], preferred_element_type=jnp.float32)
            turned = swap(both)
            one = from_tile % 2 == 0
            wanted = jnp.where(first_lanes, jnp.where(one, both, turned), jnp.where(one, turned, both))
            products[half, k] = wanted.astype(jnp.bfloat16)

    def pair_of(half, pair, i):
        one, two = PAIRS[half][pair]
        return jnp.where(first_lanes, products[half, code[i, one] // 2], products[half, code[i, two] // 2])

    def send_ring(half):
        for pair in range(2):
            for i, (dy, dc) in enumerate(OTHERS):
                ring_out[half, pair, i] = pair_of(half, pair, i)
                send(
                    ring_out.at[half, pair, i],
                    ring_in.at[half, pair, i],
                    ring_send.at[half, pair, i],
                    ring_recv.at[half, pair, i],
                    in_col(dy, 0, dc),
                )

    gather_end(0)
    multiply(0)
    send_ring(0)
    gather_end(1)
    multiply(1)
    send_ring(1)

    nodes = 2 * TILE
    place = (node_order[...] % nodes)[None, :]
    wanted_rows = lax.broadcasted_iota(jnp.int32, (nodes, nodes), 0)
    moves[...] = jnp.where(wanted_rows == place, 1.0, 0.0).astype(jnp.bfloat16)

    for i in range(len(OTHERS)):
        arrived(flags_in.at[i], flags_recv.at[i])

    def sum_ring(half, pair):
        at = 2 * half + pair
        tile = pair_of(half, pair, MINE).astype(jnp.float32)
        second = flags_out[MINE, pl.ds(at, 1), :] > 0.5
        sums = [jnp.where(second, 0.0, tile), jnp.where(second, tile, 0.0)]
        for i in range(len(OTHERS)):
            arrived(ring_in.at[half, pair, i], ring_recv.at[half, pair, i])
            tile = ring_in[half, pair, i].astype(jnp.float32)
            second = flags_in[i, pl.ds(at, 1), :] > 0.5
            sums = [sums[0] + jnp.where(second, 0.0, tile), sums[1] + jnp.where(second, tile, 0.0)]
        return jnp.where(first_lanes, sums[0], swap(sums[1])), jnp.where(first_lanes, swap(sums[0]), sums[1])

    def send_sums(half, what, value):
        sums_out[half, what] = value.astype(jnp.bfloat16)
        way, back = WAYS[half]
        send(
            sums_out.at[half, what],
            sums_in.at[half, what],
            sums_send.at[half, what],
            sums_recv.at[half, what],
            in_col(0, back if what == DIRECT else way, 0),
        )

    def sums_from(half, what):
        arrived(sums_in.at[half, what], sums_recv.at[half, what])
        return sums_in[half, what].astype(jnp.float32)

    far, beside_a = sum_ring(0, 0)
    send_sums(0, FAR, far)
    direct, own_a = sum_ring(0, 1)
    send_sums(0, DIRECT, direct)
    far, beside_b = sum_ring(1, 0)
    send_sums(1, FAR, far)
    send_sums(0, SUM, beside_a + sums_from(0, FAR))
    direct, own_b = sum_ring(1, 1)
    send_sums(1, DIRECT, direct)
    send_sums(1, SUM, beside_b + sums_from(1, FAR))
    own_a = own_a + sums_from(0, DIRECT) + sums_from(0, SUM)
    own_b = own_b + sums_from(1, DIRECT) + sums_from(1, SUM)

    low = jnp.concatenate(
        [jnp.where(first_lanes, own_a, swap(own_b)), jnp.where(first_lanes, swap(own_a), own_b)], axis=0
    ).astype(jnp.bfloat16)
    mixed = jnp.maximum(jnp.dot(low, weight[...], preferred_element_type=jnp.float32), 0.0).astype(jnp.bfloat16)
    out[...] = jnp.dot(moves[...], mixed, preferred_element_type=jnp.float32).astype(jnp.bfloat16)

    for copy in pending:
        copy.wait_send()


def on_device(features, weight, tile_values, tile_rows, tile_cols, tile_count, node_order):
    dma = pltpu.SemaphoreType.DMA
    others = len(OTHERS)
    low = jnp.bfloat16
    return pl.pallas_call(
        kernel,
        out_shape=jax.ShapeDtypeStruct(features.shape, features.dtype),
        in_specs=[pl.BlockSpec(memory_space=pltpu.HBM)] * 7,
        out_specs=pl.BlockSpec(memory_space=pltpu.VMEM),
        scratch_shapes=[
            pltpu.VMEM((2, TILE, TILE), low),
            pltpu.VMEM(weight.shape, low),
            pltpu.VMEM((SLOTS, TILE, TILE), low),
            pltpu.SMEM(tile_rows.shape, jnp.int32),
            pltpu.SMEM(tile_cols.shape, jnp.int32),
            pltpu.SMEM(tile_count.shape, jnp.int32),
            pltpu.VMEM(node_order.shape, jnp.int32),
            pltpu.VMEM((CELLS, TILE, TILE), low),
            pltpu.VMEM((CELLS, TILE, TILE), low),
            pltpu.VMEM((2, SLOTS + 1, TILE, TILE), low),
            pltpu.VMEM((2 * TILE, 2 * TILE), low),
            pltpu.VMEM((others + 1, 8, TILE), jnp.float32),
            pltpu.VMEM((others, 8, TILE), jnp.float32),
            pltpu.VMEM((2, 2, others, TILE, TILE), low),
            pltpu.VMEM((2, 2, others, TILE, TILE), low),
            pltpu.VMEM((2, 3, TILE, TILE), low),
            pltpu.VMEM((2, 3, TILE, TILE), low),
            dma((7,)),
            dma((30,)),
            dma((2, CELLS)),
            dma((others,)),
            dma((others,)),
            dma((2, 2, others)),
            dma((2, 2, others)),
            dma((2, 3)),
            dma((2, 3)),
        ],
        compiler_params=pltpu.CompilerParams(
            collective_id=0, has_side_effects=True, vmem_limit_bytes=60 * 2**20
        ),
        name="graph_convolution",
    )(features.reshape(2, TILE, TILE), weight, tile_values, tile_rows, tile_cols, tile_count, node_order)


def solution(mesh):
    return jax.shard_map(
        on_device,
        mesh=mesh,
        in_specs=(
            P(("col", "row"), None),
            P(),
            P("row", "col", None, None, None),
            P("row", "col", None),
            P("row", "col", None),
            P("row", "col"),
            P(("row", "col")),
        ),
        out_specs=P(("row", "col"), None),
        check_vma=False,
    )
```

time: 259 us -> 54.8 us (0.21)
  waiting for transfers between devices: 229 us -> 0 us
  Pallas kernels: 0 us -> 52.5 us
  between operations: 14.1 us -> 0.66 us
  local copies, waits for them, and re-layouts: 9.49 us -> 1.47 us
  matrix products: 5.59 us -> 0 us
    reduce_scatter x1 -> x0, waiting for transfers between devices: 146 us -> none  [on_device(): lax.psum_scatter(summed.reshape(whole_tiles * tile_size, feature_width),...]
    all_gather x1 -> x0, waiting for transfers between devices: 82.4 us -> none  [on_device(): gathered = lax.all_gather(features, 'row', axis=0, tiled=True)]
    pallas_call x0 -> x1, Pallas kernels: none -> 52.5 us  [on_device(): pl.pallas_call(kernel, out_shape=jax.ShapeDtypeStruct(features.shape, fea...]
    dot_general x3 -> x0, matrix products: 5.59 us -> none  [the longest x1 4.03 us: on_device(): jnp.dot(onehot, products, precision=lax.Precision.HIGHEST, preferred_elem...]
    reshape x1 -> x0, local copies, waits for them, and re-layouts: 4.87 us -> none  [on_device(): summed.reshape(whole_tiles * tile_size, feature_width)]
  transfers between devices with their start and end apart: 2 -> 0, of which waited for: 2 -> 0; matrix products, arithmetic and copies ran while one was open for 0% -> 0% of each run, Pallas kernels for 0% -> 0%
where the time goes in v2:
time: 54.8 us; the launch traced here: 54.6 us
  Pallas kernels  52.5 us (96%)
  local copies, waits for them, and re-layouts  1.47 us (3%)
  between operations  0.66 us (1%)
    pallas_call x1, Pallas kernels, on_device(): pl.pallas_call(kernel, out_shape=jax.ShapeDtypeStruct(features.shape, fea...  52.5 us
    unnamed x1, local copies, waits for them, and re-layouts  1.47 us

profile of v2, /device:TPU:1, one launch (start us, length us, event | category | flops | bytes accessed | tf_op | source)
XLA Modules:
  0.0 54.6 jit_solution(8636286928383819403)
XLA Ops:
  0.7 52.5 %graph_convolution.1 = bf16[256,128]{1,0:T(8,128)(2,1)} custom-call(bf16[2,128,128]{2,1,0:T(8,128)(2,1)} %bitcast.1, bf16[128,128]{1,0:T(8,128)(2,1)} %weight_hbm.1, bf16[1,1,16,128,128]{4,3,2,1,0:T(8,128)(2,1)} %tile_values_hbm.1, s32[1,1,16]{2,1,0:T(1,128)} %tile_rows_hbm.1, s32[1,1,16]{2,1,0:T(1,128)} %tile_cols_hbm.1, s32[1,1]{1,0:T(1,128)S(6)} %copy.9.tile_count_hbm, ...), custom_call_target="tpu_custom_call" | custom-call | tf_op jit(solution)/shard_map/graph_convolution/pallas_call | solution.py:277
  53.1 1.5 %copy.10 = bf16[256,128]{1,0:T(8,128)(2,1)} copy(bf16[256,128]{1,0:T(8,128)(2,1)} %graph_convolution.1) | data formatting | bytes 131072

commit v3 on v2

--- a/solution.py
+++ b/solution.py
@@ -14,9 +14,7 @@
 RING = tuple((dy, dc) for dy in (2, 1, 3, 0) for dc in (1, 0))
 OTHERS = RING[:-1]
 MINE = len(OTHERS)
-WAYS = ((1, 3), (3, 1))
-PAIRS = tuple(((2, way), (back, 0)) for way, back in WAYS)
-FAR, SUM, DIRECT = range(3)
+PAIRS = ((2, 1), (3, 0))
 
 
 def kernel(
@@ -54,6 +52,7 @@
     ring_recv,
     sums_send,
     sums_recv,
+    far_sem,
 ):
     row, col = lax.axis_index("row"), lax.axis_index("col")
     z, x = row // LINE, row % LINE
@@ -147,6 +146,11 @@
     send_along_z(0)
     send_along_x(0, z)
     send_along_z(1)
+    pl.semaphore_signal(far_sem, inc=1, device_id=in_col(0, 3, 0), device_id_type=MESH)
+
+    forward(0)
+    send_along_x(1, z)
+    forward(1)
 
     for load in loads[1:4]:
         load.wait()
@@ -161,20 +165,15 @@
             code = jnp.where(owners[k] == owner, codes[k], code)
         return code
 
-    forward(0)
-    send_along_x(1, z)
-
     code = {(i, dh): code_of(dy, dh, dc) for i, (dy, dc) in enumerate(RING) for dh in range(LINE)}
     lanes = lax.broadcasted_iota(jnp.int32, (1, TILE), 1) < HALF
     for i in range(len(RING)):
         for half in range(2):
-            for pair, (one, two) in enumerate(PAIRS[half]):
+            for pair, (one, two) in enumerate(PAIRS):
                 second = jnp.where(lanes, code[i, one] % 2, code[i, two] % 2).astype(jnp.float32)
                 flags_out[i, pl.ds(2 * half + pair, 1), :] = second
     for i, (dy, dc) in enumerate(OTHERS):
         send(flags_out.at[i], flags_in.at[i], flags_send.at[i], flags_recv.at[i], in_col(dy, 0, dc))
-
-    forward(1)
 
     for load in loads[4:]:
         load.wait()
@@ -190,7 +189,7 @@
             products[half, k] = wanted.astype(jnp.bfloat16)
 
     def pair_of(half, pair, i):
-        one, two = PAIRS[half][pair]
+        one, two = PAIRS[pair]
         return jnp.where(first_lanes, products[half, code[i, one] // 2], products[half, code[i, two] // 2])
 
     def send_ring(half):
@@ -232,33 +231,30 @@
             sums = [sums[0] + jnp.where(second, 0.0, tile), sums[1] + jnp.where(second, tile, 0.0)]
         return jnp.where(first_lanes, sums[0], swap(sums[1])), jnp.where(first_lanes, swap(sums[0]), sums[1])
 
-    def send_sums(half, what, value):
-        sums_out[half, what] = value.astype(jnp.bfloat16)
-        way, back = WAYS[half]
+    def send_sums(half, dh, value):
+        sums_out[half, dh - 1] = value.astype(jnp.bfloat16)
         send(
-            sums_out.at[half, what],
-            sums_in.at[half, what],
-            sums_send.at[half, what],
-            sums_recv.at[half, what],
-            in_col(0, back if what == DIRECT else way, 0),
+            sums_out.at[half, dh - 1],
+            sums_in.at[half, dh - 1],
+            sums_send.at[half, dh - 1],
+            sums_recv.at[half, dh - 1],
+            in_col(0, dh, 0),
         )
 
-    def sums_from(half, what):
-        arrived(sums_in.at[half, what], sums_recv.at[half, what])
-        return sums_in[half, what].astype(jnp.float32)
-
-    far, beside_a = sum_ring(0, 0)
-    send_sums(0, FAR, far)
-    direct, own_a = sum_ring(0, 1)
-    send_sums(0, DIRECT, direct)
-    far, beside_b = sum_ring(1, 0)
-    send_sums(1, FAR, far)
-    send_sums(0, SUM, beside_a + sums_from(0, FAR))
-    direct, own_b = sum_ring(1, 1)
-    send_sums(1, DIRECT, direct)
-    send_sums(1, SUM, beside_b + sums_from(1, FAR))
-    own_a = own_a + sums_from(0, DIRECT) + sums_from(0, SUM)
-    own_b = own_b + sums_from(1, DIRECT) + sums_from(1, SUM)
+    pl.semaphore_wait(far_sem, 1)
+    own = []
+    for half in range(2):
+        far, near_sum = sum_ring(half, 0)
+        send_sums(half, 2, far)
+        send_sums(half, 1, near_sum)
+        near_sum, mine = sum_ring(half, 1)
+        send_sums(half, 3, near_sum)
+        own.append(mine)
+    for half in range(2):
+        for dh in (1, 3, 2):
+            arrived(sums_in.at[half, dh - 1], sums_recv.at[half, dh - 1])
+            own[half] = own[half] + sums_in[half, dh - 1].astype(jnp.float32)
+    own_a, own_b = own
 
     low = jnp.concatenate(
         [jnp.where(first_lanes, own_a, swap(own_b)), jnp.where(first_lanes, swap(own_a), own_b)], axis=0
@@ -274,9 +270,10 @@
     dma = pltpu.SemaphoreType.DMA
     others = len(OTHERS)
     low = jnp.bfloat16
+    operands = (features.reshape(2, TILE, TILE), weight, tile_values, tile_rows, tile_cols, tile_count, node_order)
     return pl.pallas_call(
         kernel,
-        out_shape=jax.ShapeDtypeStruct(features.shape, features.dtype),
+        out_shape=pltpu.VMEM(features.shape, features.dtype),
         in_specs=[pl.BlockSpec(memory_space=pltpu.HBM)] * 7,
         out_specs=pl.BlockSpec(memory_space=pltpu.VMEM),
         scratch_shapes=[
@@ -306,12 +303,15 @@
             dma((2, 2, others)),
             dma((2, 3)),
             dma((2, 3)),
+            pltpu.SemaphoreType.REGULAR,
         ],
         compiler_params=pltpu.CompilerParams(
-            collective_id=0, has_side_effects=True, vmem_limit_bytes=60 * 2**20
+            collective_id=0, has_side_effects=True, vmem_limit_bytes=32 * 2**20
         ),
         name="graph_convolution",
-    )(features.reshape(2, TILE, TILE), weight, tile_values, tile_rows, tile_cols, tile_count, node_order)
+    )(
+        *(operand if operand is tile_count else pltpu.with_memory_space_constraint(operand, pltpu.HBM) for operand in operands)
+    )
 
 
 def solution(mesh):

time: 54.8 us -> 51 us (0.931)
  Pallas kernels: 52.5 us -> 49.5 us
  local copies, waits for them, and re-layouts: 1.47 us -> 0.63 us
    pallas_call x1, Pallas kernels: 52.5 us -> 49.5 us  [on_device(): pl.pallas_call(kernel, out_shape=pltpu.VMEM(features.shape, features.dtyp...]
    unnamed x1, local copies, waits for them, and re-layouts: 1.47 us -> 0.63 us
where the time goes in v3:
time: 51 us; the launch traced here: 50.8 us
  Pallas kernels  49.5 us (97%)
  between operations  0.66 us (1%)
  local copies, waits for them, and re-layouts  0.63 us (1%)
    pallas_call x1, Pallas kernels, on_device(): pl.pallas_call(kernel, out_shape=pltpu.VMEM(features.shape, features.dtyp...  49.5 us

profile of v3, /device:TPU:1, one launch (start us, length us, event | category | flops | bytes accessed | tf_op | source)
XLA Modules:
  0.0 50.8 jit_solution(14766449451386901267)
XLA Ops:
  0.7 49.5 %graph_convolution.1 = bf16[256,128]{1,0:T(8,128)(2,1)S(1)} custom-call(bf16[2,128,128]{2,1,0:T(8,128)(2,1)} %bitcast.1, bf16[128,128]{1,0:T(8,128)(2,1)} %weight_hbm.1, bf16[1,1,16,128,128]{4,3,2,1,0:T(8,128)(2,1)} %tile_values_hbm.1, s32[1,1,16]{2,1,0:T(1,128)} %tile_rows_hbm.1, s32[1,1,16]{2,1,0:T(1,128)} %tile_cols_hbm.1, ...), custom_call_target="tpu_custom_call" | custom-call | tf_op jit(solution)/shard_map/graph_convolution/pallas_call | solution.py:274
  50.2 0.6 %copy.9 = bf16[256,128]{1,0:T(8,128)(2,1)} copy(bf16[256,128]{1,0:T(8,128)(2,1)S(1)} %graph_convolution.1) | data formatting | bytes 131072

commit v4 on v3

v4 whole, which is shorter than its diff:
```python
import jax
import jax.numpy as jnp
from jax import lax
from jax.experimental import pallas as pl
from jax.experimental.pallas import tpu as pltpu
from jax.sharding import PartitionSpec as P

MESH = pl.DeviceIdType.MESH
TILE = 128
HALF = TILE // 2
CHUNKS = 4
WIDTH = TILE // CHUNKS
SLOTS = 16
LAST = 3
LINE = 4
CELLS = LINE * LINE
RING = tuple((dy, dc) for dy in (2, 1, 3, 0) for dc in (1, 0))
OTHERS = RING[:-1]
MINE = len(OTHERS)
GROUPS = (2, 1, 3, 0)


def kernel(
    features_hbm,
    weight_hbm,
    tile_values_hbm,
    tile_rows_hbm,
    tile_cols_hbm,
    tile_count_hbm,
    node_order_hbm,
    out,
    features,
    weight,
    tiles,
    tile_rows,
    tile_cols,
    tile_count,
    node_order,
    gathered_0,
    gathered_1,
    gathered_2,
    gathered_3,
    products,
    picks,
    moves,
    flags_out,
    flags_in,
    ring_out,
    ring_in,
    sums_out,
    sums_in,
    load_sem,
    gather_send,
    gather_recv,
    flags_send,
    flags_recv,
    ring_send,
    ring_recv,
    sums_send,
    sums_recv,
    far_sem,
):
    row, col = lax.axis_index("row"), lax.axis_index("col")
    z, x = row // LINE, row % LINE
    y, h, core = col // 8, (col // 2) % LINE, col % 2
    group = lax.broadcasted_iota(jnp.int32, (TILE, TILE), 1) // WIDTH
    half_group = lax.broadcasted_iota(jnp.int32, (HALF, TILE), 1) // WIDTH

    def in_row(z_at, x_at):
        return (z_at * LINE + x_at, col)

    def in_col(dy, dh, dc):
        return (row, ((y + dy) % LINE) * 8 + ((h + dh) % LINE) * 2 + (core + dc) % 2)

    gathered = (gathered_0, gathered_1, gathered_2, gathered_3)
    pending = []

    def send(src, dst, send_sem, recv_sem, device):
        copy = pltpu.make_async_remote_copy(
            src_ref=src, dst_ref=dst, send_sem=send_sem, recv_sem=recv_sem, device_id=device, device_id_type=MESH
        )
        copy.start()
        pending.append(copy)

    def arrived(ref, sem):
        pltpu.make_async_copy(ref, ref, sem).wait()

    def by_group(groups, pieces):
        value = pieces[0]
        for m in range(1, CHUNKS):
            value = jnp.where(groups == m, pieces[m], value)
        return value

    def shift(value, groups):
        return pltpu.roll(value, groups % CHUNKS * WIDTH, 1) if groups % CHUNKS else value

    barrier = pltpu.get_barrier_semaphore()
    partners = (
        [in_row((z + d) % LINE, x) for d in (1, 2, 3)]
        + [in_row(z, (x + d) % LINE) for d in (1, 2, 3)]
        + [in_col(dy, 0, dc) for dy, dc in OTHERS]
        + [in_col(0, dh, 0) for dh in (1, 3)]
    )
    for device in partners:
        pl.semaphore_signal(barrier, inc=1, device_id=device, device_id_type=MESH)

    loads = [
        pltpu.make_async_copy(src, dst, load_sem.at[i])
        for i, (src, dst) in enumerate(
            (
                (features_hbm, features),
                (tile_rows_hbm, tile_rows),
                (tile_cols_hbm, tile_cols),
                (tile_count_hbm, tile_count),
                (tile_values_hbm.at[0, 0], tiles),
                (node_order_hbm, node_order),
                (weight_hbm, weight),
            )
        )
    ]
    for load in loads:
        load.start()

    from_lane = lax.broadcasted_iota(jnp.int32, (TILE, 2 * TILE), 0)
    to_lane = lax.broadcasted_iota(jnp.int32, (TILE, 2 * TILE), 1)
    for s in range(2):
        wanted_lane = (2 * s + to_lane // TILE) * WIDTH + to_lane % WIDTH
        picks[s] = jnp.where(from_lane == wanted_lane, 1.0, 0.0).astype(jnp.bfloat16)

    loads[0].wait()
    quarters = [features[m // 2, pl.ds(m % 2 * HALF, HALF), :].astype(jnp.float32) for m in range(CHUNKS)]
    for c in range(CHUNKS):
        gathered[c][row] = by_group(half_group, [shift(quarters[m], m - c) for m in range(CHUNKS)]).astype(jnp.bfloat16)
    pl.semaphore_wait(barrier, len(partners))

    sends = [0]

    def send_block(c, slot, device):
        block = gathered[c].at[slot]
        send(block, block, gather_send.at[sends[0]], gather_recv.at[c, slot], device)
        sends[0] += 1

    def send_along_z(c, x_from):
        for d in (1, 3, 2):
            send_block(c, z * LINE + x_from, in_row((z + d) % LINE, x))

    def send_along_x(c, z_from):
        for d in (2, 1, 3):
            send_block(c, z_from * LINE + x, in_row(z, (x + d) % LINE))

    def block_arrived(c, slot):
        arrived(gathered[c].at[slot], gather_recv.at[c, slot])

    near = [jnp.where(z % 2 == 0, z + 1, z - 1), jnp.where(z < 2, 2, 1), jnp.where(z < 2, 3, 0)]

    def forward(c):
        for z_from in near:
            block_arrived(c, z_from * LINE + x)
            send_along_x(c, z_from)

    def forward_last():
        send_along_z(LAST, x)
        for d in (1, 3, 2):
            x_from = (x + d) % LINE
            block_arrived(LAST, z * LINE + x_from)
            send_along_z(LAST, x_from)

    def gather_end(c):
        for z_from in [z] + near if c != LAST else near:
            for d in (1, 3, 2) if c != LAST else (0, 1, 3, 2):
                block_arrived(c, z_from * LINE + (x + d) % LINE)

    send_along_z(0, x)
    send_along_x(0, z)
    send_along_x(LAST, z)
    send_along_z(1, x)
    send_along_z(2, x)
    pl.semaphore_signal(far_sem, inc=1, device_id=in_col(0, 3, 0), device_id_type=MESH)

    for load in loads[1:4]:
        load.wait()
    count = tile_count[0, 0]
    owners = [jnp.where(k < count, tile_rows[0, 0, k] // 2, -1) for k in range(SLOTS)]
    codes = [2 * k + tile_rows[0, 0, k] % 2 for k in range(SLOTS)]

    def code_of(dy, dh, dc):
        owner = in_col(dy, dh, dc)[1]
        code = 2 * SLOTS
        for k in range(SLOTS):
            code = jnp.where(owners[k] == owner, codes[k], code)
        return code

    code = {(i, dh): code_of(dy, dh, dc) for i, (dy, dc) in enumerate(RING) for dh in range(LINE)}
    row_group = lax.broadcasted_iota(jnp.int32, (1, TILE), 1) // WIDTH
    for i in range(len(RING)):
        second = by_group(row_group, [code[i, dh] % 2 for dh in GROUPS])
        flags_out[i, pl.ds(0, 1), :] = second.astype(jnp.float32)
    for i, (dy, dc) in enumerate(OTHERS):
        send(flags_out.at[i], flags_in.at[i], flags_send.at[i], flags_recv.at[i], in_col(dy, 0, dc))

    forward(0)
    send_along_x(1, z)
    forward_last()
    forward(1)
    send_along_x(2, z)
    forward(2)

    nodes = 2 * TILE
    for load in loads[4:]:
        load.wait()
    place = (node_order[...] % nodes)[None, :]
    wanted_rows = lax.broadcasted_iota(jnp.int32, (nodes, nodes), 0)
    moves[...] = jnp.where(wanted_rows == place, 1.0, 0.0).astype(jnp.bfloat16)

    def multiply(c):
        products[c, SLOTS] = jnp.zeros((TILE, TILE), jnp.bfloat16)
        for k in range(SLOTS):
            tile = tile_cols[0, 0, k]
            picked = jnp.dot(gathered[c][tile // 2], picks[tile % 2], preferred_element_type=jnp.float32)
            inputs = jnp.concatenate([picked[:, :TILE], picked[:, TILE:]], axis=0).astype(jnp.bfloat16)
            products[c, k] = jnp.dot(tiles[k], inputs, preferred_element_type=jnp.float32).astype(jnp.bfloat16)

    def tiles_for(c, i):
        return by_group(group, [products[c, code[i, dh] // 2] for dh in GROUPS])

    def send_ring(c):
        gather_end(c)
        multiply(c)
        for i, (dy, dc) in enumerate(OTHERS):
            ring_out[c, i] = tiles_for(c, i)
            send(ring_out.at[c, i], ring_in.at[c, i], ring_send.at[c, i], ring_recv.at[c, i], in_col(dy, 0, dc))

    def sum_ring(c):
        tile = tiles_for(c, MINE).astype(jnp.float32)
        second = flags_out[MINE, pl.ds(0, 1), :] > 0.5
        sums = [jnp.where(second, 0.0, tile), jnp.where(second, tile, 0.0)]
        for i in range(len(OTHERS)):
            arrived(ring_in.at[c, i], ring_recv.at[c, i])
            tile = ring_in[c, i].astype(jnp.float32)
            second = flags_in[i, pl.ds(0, 1), :] > 0.5
            sums = [sums[0] + jnp.where(second, 0.0, tile), sums[1] + jnp.where(second, tile, 0.0)]
        rows = [sums[m // 2][m % 2 * HALF : m % 2 * HALF + HALF] for m in range(CHUNKS)]
        return [by_group(half_group, [shift(rows[m], m - g) for m in range(CHUNKS)]) for g in range(LINE)]

    own = []

    def send_sums(c):
        sums = sum_ring(c)
        for g, dh in enumerate(GROUPS[:-1]):
            sums_out[c, g] = sums[g].astype(jnp.bfloat16)
            send(sums_out.at[c, g], sums_in.at[c, g], sums_send.at[c, g], sums_recv.at[c, g], in_col(0, dh, 0))
        own.append(sums[-1])

    send_ring(0)
    send_ring(1)
    send_ring(2)
    for i in range(len(OTHERS)):
        arrived(flags_in.at[i], flags_recv.at[i])
    pl.semaphore_wait(far_sem, 1)
    send_sums(0)
    send_ring(3)
    send_sums(1)
    send_sums(2)
    send_sums(3)
    for c in range(CHUNKS):
        for g in (1, 2, 0):
            arrived(sums_in.at[c, g], sums_recv.at[c, g])
            own[c] = own[c] + sums_in[c, g].astype(jnp.float32)

    low = jnp.concatenate(
        [by_group(half_group, [shift(own[c], c - m) for c in range(CHUNKS)]) for m in range(CHUNKS)], axis=0
    ).astype(jnp.bfloat16)
    mixed = jnp.maximum(jnp.dot(low, weight[...], preferred_element_type=jnp.float32), 0.0).astype(jnp.bfloat16)
    out[...] = jnp.dot(moves[...], mixed, preferred_element_type=jnp.float32).astype(jnp.bfloat16)

    for copy in pending:
        copy.wait_send()


def on_device(features, weight, tile_values, tile_rows, tile_cols, tile_count, node_order):
    dma = pltpu.SemaphoreType.DMA
    others = len(OTHERS)
    low = jnp.bfloat16
    operands = (features.reshape(2, TILE, TILE), weight, tile_values, tile_rows, tile_cols, tile_count, node_order)
    return pl.pallas_call(
        kernel,
        out_shape=pltpu.VMEM(features.shape, features.dtype),
        in_specs=[pl.BlockSpec(memory_space=pltpu.HBM)] * 7,
        out_specs=pl.BlockSpec(memory_space=pltpu.VMEM),
        scratch_shapes=[
            pltpu.VMEM((2, TILE, TILE), low),
            pltpu.VMEM(weight.shape, low),
            pltpu.VMEM((SLOTS, TILE, TILE), low),
            pltpu.SMEM(tile_rows.shape, jnp.int32),
            pltpu.SMEM(tile_cols.shape, jnp.int32),
            pltpu.SMEM(tile_count.shape, jnp.int32),
            pltpu.VMEM(node_order.shape, jnp.int32),
            *[pltpu.VMEM((CELLS, HALF, TILE), low)] * CHUNKS,
            pltpu.VMEM((CHUNKS, SLOTS + 1, TILE, TILE), low),
            pltpu.VMEM((2, TILE, 2 * TILE), low),
            pltpu.VMEM((2 * TILE, 2 * TILE), low),
            pltpu.VMEM((others + 1, 8, TILE), jnp.float32),
            pltpu.VMEM((others, 8, TILE), jnp.float32),
            pltpu.VMEM((CHUNKS, others, TILE, TILE), low),
            pltpu.VMEM((CHUNKS, others, TILE, TILE), low),
            pltpu.VMEM((CHUNKS, LINE - 1, HALF, TILE), low),
            pltpu.VMEM((CHUNKS, LINE - 1, HALF, TILE), low),
            dma((7,)),
            dma((60,)),
            dma((CHUNKS, CELLS)),
            dma((others,)),
            dma((others,)),
            dma((CHUNKS, others)),
            dma((CHUNKS, others)),
            dma((CHUNKS, LINE - 1)),
            dma((CHUNKS, LINE - 1)),
            pltpu.SemaphoreType.REGULAR,
        ],
        compiler_params=pltpu.CompilerParams(
            collective_id=0, has_side_effects=True, vmem_limit_bytes=32 * 2**20
        ),
        name="graph_convolution",
    )(
        *(operand if operand is tile_count else pltpu.with_memory_space_constraint(operand, pltpu.HBM) for operand in operands)
    )


def solution(mesh):
    return jax.shard_map(
        on_device,
        mesh=mesh,
        in_specs=(
            P(("col", "row"), None),
            P(),
            P("row", "col", None, None, None),
            P("row", "col", None),
            P("row", "col", None),
            P("row", "col"),
            P(("row", "col")),
        ),
        out_specs=P(("row", "col"), None),
        check_vma=False,
    )
```

time: 51 us -> 48.7 us (0.955)
  the two profiles are of different devices: /device:TPU:1 before, /device:TPU:32 now
where the time goes in v4:
time: 48.7 us; the launch traced here: 48.5 us
  Pallas kernels  47.2 us (97%)
  between operations  0.66 us (1%)
  local copies, waits for them, and re-layouts  0.63 us (1%)
    pallas_call x1, Pallas kernels, on_device(): pl.pallas_call(kernel, out_shape=pltpu.VMEM(features.shape, features.dtyp...  47.2 us

profile of v4, /device:TPU:32, one launch (start us, length us, event | category | flops | bytes accessed | tf_op | source)
XLA Modules:
  0.0 48.5 jit_solution(15862508967926200879)
XLA Ops:
  0.7 47.2 %graph_convolution.1 = bf16[256,128]{1,0:T(8,128)(2,1)S(1)} custom-call(bf16[2,128,128]{2,1,0:T(8,128)(2,1)} %bitcast.1, bf16[128,128]{1,0:T(8,128)(2,1)} %weight_hbm.1, bf16[1,1,16,128,128]{4,3,2,1,0:T(8,128)(2,1)} %tile_values_hbm.1, s32[1,1,16]{2,1,0:T(1,128)} %tile_rows_hbm.1, s32[1,1,16]{2,1,0:T(1,128)} %tile_cols_hbm.1, ...), custom_call_target="tpu_custom_call" | custom-call | tf_op jit(solution)/shard_map/graph_convolution/pallas_call | solution.py:285
  47.9 0.6 %copy.9 = bf16[256,128]{1,0:T(8,128)(2,1)} copy(bf16[256,128]{1,0:T(8,128)(2,1)S(1)} %graph_convolution.1) | data formatting | bytes 131072

commit v5 on v4

v5 whole, which is shorter than its diff:
```python
import jax
import jax.numpy as jnp
from jax import lax
from jax.experimental import pallas as pl
from jax.experimental.pallas import tpu as pltpu
from jax.sharding import PartitionSpec as P

MESH = pl.DeviceIdType.MESH
TILE = 128
HALF = TILE // 2
CHUNKS = 4
WIDTH = TILE // CHUNKS
FLAG_ROWS = 16
SLOTS = 16
LAST = 3
LINE = 4
CELLS = LINE * LINE
RING = tuple((dy, dc) for dy in (2, 1, 3, 0) for dc in (1, 0))
OTHERS = RING[:-1]
MINE = len(OTHERS)
GROUPS = (2, 1, 3, 0)


def kernel(
    features_hbm,
    weight_hbm,
    tile_values_hbm,
    tile_rows_hbm,
    tile_cols_hbm,
    tile_count_hbm,
    node_order_hbm,
    out,
    features,
    weight,
    tiles,
    tile_rows,
    tile_cols,
    tile_count,
    node_order,
    gathered_0,
    gathered_1,
    gathered_2,
    gathered_3,
    products,
    picks,
    moves,
    ring_out,
    ring_in,
    sums_out,
    sums_in,
    load_sem,
    gather_send,
    gather_recv,
    ring_send,
    ring_recv,
    sums_send,
    sums_recv,
    far_sem,
):
    row, col = lax.axis_index("row"), lax.axis_index("col")
    z, x = row // LINE, row % LINE
    y, h, core = col // 8, (col // 2) % LINE, col % 2
    group = lax.broadcasted_iota(jnp.int32, (TILE, TILE), 1) // WIDTH
    half_group = lax.broadcasted_iota(jnp.int32, (HALF, TILE), 1) // WIDTH

    def in_row(z_at, x_at):
        return (z_at * LINE + x_at, col)

    def in_col(dy, dh, dc):
        return (row, ((y + dy) % LINE) * 8 + ((h + dh) % LINE) * 2 + (core + dc) % 2)

    def slot_of(c, row_at):
        return row_at if c == LAST else row_at % LINE * LINE + row_at // LINE

    gathered = (gathered_0, gathered_1, gathered_2, gathered_3)
    def send(src, dst, send_sem, recv_sem, device):
        copy = pltpu.make_async_remote_copy(
            src_ref=src, dst_ref=dst, send_sem=send_sem, recv_sem=recv_sem, device_id=device, device_id_type=MESH
        )
        copy.start()

    def arrived(ref, sem):
        pltpu.make_async_copy(ref, ref, sem).wait()

    def by_group(groups, pieces):
        value = pieces[0]
        for m in range(1, CHUNKS):
            value = jnp.where(groups == m, pieces[m], value)
        return value

    def shift(value, groups):
        return pltpu.roll(value, groups % CHUNKS * WIDTH, 1) if groups % CHUNKS else value

    barrier = pltpu.get_barrier_semaphore()
    partners = (
        [in_row((z + d) % LINE, x) for d in (1, 2, 3)]
        + [in_row(z, (x + d) % LINE) for d in (1, 2, 3)]
        + [in_col(dy, 0, dc) for dy, dc in OTHERS]
        + [in_col(0, dh, 0) for dh in (1, 3)]
    )
    for device in partners:
        pl.semaphore_signal(barrier, inc=1, device_id=device, device_id_type=MESH)

    loads = [
        pltpu.make_async_copy(src, dst, load_sem.at[i])
        for i, (src, dst) in enumerate(
            (
                (features_hbm, features),
                (tile_rows_hbm, tile_rows),
                (tile_cols_hbm, tile_cols),
                (tile_count_hbm, tile_count),
                (tile_values_hbm.at[0, 0], tiles),
                (node_order_hbm, node_order),
                (weight_hbm, weight),
            )
        )
    ]
    for load in loads:
        load.start()

    from_lane = lax.broadcasted_iota(jnp.int32, (TILE, 2 * TILE), 0)
    to_lane = lax.broadcasted_iota(jnp.int32, (TILE, 2 * TILE), 1)
    for s in range(2):
        wanted_lane = (2 * s + to_lane // TILE) * WIDTH + to_lane % WIDTH
        picks[s] = jnp.where(from_lane == wanted_lane, 1.0, 0.0).astype(jnp.bfloat16)

    loads[0].wait()
    quarters = [features[m // 2, pl.ds(m % 2 * HALF, HALF), :].astype(jnp.float32) for m in range(CHUNKS)]
    for c in range(CHUNKS):
        gathered[c][slot_of(c, row)] = by_group(half_group, [shift(quarters[m], m - c) for m in range(CHUNKS)]).astype(jnp.bfloat16)
    pl.semaphore_wait(barrier, len(partners))

    def send_mine(c):
        mine = gathered[c].at[slot_of(c, row)]
        for d in (2, 1, 3) if c == LAST else (1, 3, 2):
            to = in_row(z, (x + d) % LINE) if c == LAST else in_row((z + d) % LINE, x)
            send(mine, mine, gather_send.at[c, 0], gather_recv.at[c, 0], to)

    def forward(c):
        arrived(gathered[c].at[pl.ds(0, LINE - 1)], gather_recv.at[c, 0])
        line = gathered[c].at[pl.ds(slot_of(c, row) // LINE * LINE, LINE)]
        for d in (1, 3, 2) if c == LAST else (2, 1, 3):
            to = in_row((z + d) % LINE, x) if c == LAST else in_row(z, (x + d) % LINE)
            send(line, line, gather_send.at[c, 1], gather_recv.at[c, 1], to)

    def mine_sent(c):
        arrived(gathered[c].at[pl.ds(0, LINE - 1)], gather_send.at[c, 0])

    def line_sent(c):
        arrived(gathered[c].at[pl.ds(0, CELLS - LINE)], gather_send.at[c, 1])

    def gather_end(c):
        arrived(gathered[c].at[pl.ds(0, CELLS - LINE)], gather_recv.at[c, 1])

    send_mine(0)
    send_mine(3)
    send_mine(1)
    send_mine(2)
    pl.semaphore_signal(far_sem, inc=1, device_id=in_col(0, 3, 0), device_id_type=MESH)

    for load in loads[1:4]:
        load.wait()
    count = tile_count[0, 0]
    owners = [jnp.where(k < count, tile_rows[0, 0, k] // 2, -1) for k in range(SLOTS)]
    codes = [2 * k + tile_rows[0, 0, k] % 2 for k in range(SLOTS)]

    def code_of(dy, dh, dc):
        owner = in_col(dy, dh, dc)[1]
        code = 2 * SLOTS
        for k in range(SLOTS):
            code = jnp.where(owners[k] == owner, codes[k], code)
        return code

    code = {(i, dh): code_of(dy, dh, dc) for i, (dy, dc) in enumerate(RING) for dh in range(LINE)}
    row_group = lax.broadcasted_iota(jnp.int32, (FLAG_ROWS, TILE), 1) // WIDTH

    def flags_for(i):
        return by_group(row_group, [code[i, dh] % 2 for dh in GROUPS]).astype(jnp.float32)

    for i in range(len(OTHERS)):
        ring_out[0, i, pl.ds(TILE, FLAG_ROWS), :] = flags_for(i).astype(jnp.bfloat16)


    def multiply(c):
        products[c, SLOTS] = jnp.zeros((TILE, TILE), jnp.bfloat16)
        for k in range(SLOTS):
            tile = tile_cols[0, 0, k]
            picked = jnp.dot(gathered[c][slot_of(c, tile // 2)], picks[tile % 2], preferred_element_type=jnp.float32)
            inputs = jnp.concatenate([picked[:, :TILE], picked[:, TILE:]], axis=0).astype(jnp.bfloat16)
            products[c, k] = jnp.dot(tiles[k], inputs, preferred_element_type=jnp.float32).astype(jnp.bfloat16)

    def tiles_for(c, i):
        return by_group(group, [products[c, code[i, dh] // 2] for dh in GROUPS])

    def ring_rows(c):
        return pl.ds(0, TILE + FLAG_ROWS if c == 0 else TILE)

    def send_ring(c):
        gather_end(c)
        multiply(c)
        rows = ring_rows(c)
        for i, (dy, dc) in enumerate(OTHERS):
            ring_out[c, i, pl.ds(0, TILE), :] = tiles_for(c, i)
            send(ring_out.at[c, i, rows], ring_in.at[c, i, rows], ring_send.at[c], ring_recv.at[c], in_col(dy, 0, dc))

    def ring_sent(c):
        arrived(ring_out.at[c, :, ring_rows(c)], ring_send.at[c])

    def sum_ring(c):
        tile = tiles_for(c, MINE).astype(jnp.float32)
        second = flags_for(MINE)[:1] > 0.5
        sums = [jnp.where(second, 0.0, tile), jnp.where(second, tile, 0.0)]
        arrived(ring_in.at[c, :, ring_rows(c)], ring_recv.at[c])
        for i in range(len(OTHERS)):
            tile = ring_in[c, i, pl.ds(0, TILE), :].astype(jnp.float32)
            second = ring_in[0, i, pl.ds(TILE, FLAG_ROWS), :].astype(jnp.float32)[:1] > 0.5
            sums = [sums[0] + jnp.where(second, 0.0, tile), sums[1] + jnp.where(second, tile, 0.0)]
        rows = [sums[m // 2][m % 2 * HALF : m % 2 * HALF + HALF] for m in range(CHUNKS)]
        return [by_group(half_group, [shift(rows[m], m - g) for m in range(CHUNKS)]) for g in range(LINE)]

    own = []

    def send_sums(c):
        sums = sum_ring(c)
        for g, dh in enumerate(GROUPS[:-1]):
            sums_out[c, g] = sums[g].astype(jnp.bfloat16)
            send(sums_out.at[c, g], sums_in.at[c, g], sums_send.at[c], sums_recv.at[c], in_col(0, dh, 0))
        own.append(sums[-1])

    forward(0)
    forward(3)
    forward(1)
    forward(2)
    loads[4].wait()
    send_ring(0)
    pl.semaphore_wait(far_sem, 1)
    send_ring(1)
    send_sums(0)
    send_ring(2)
    send_ring(3)
    send_sums(1)
    send_sums(2)
    nodes = 2 * TILE
    for load in loads[5:]:
        load.wait()
    place = (node_order[...] % nodes)[None, :]
    wanted_rows = lax.broadcasted_iota(jnp.int32, (nodes, nodes), 0)
    moves[...] = jnp.where(wanted_rows == place, 1.0, 0.0).astype(jnp.bfloat16)
    send_sums(3)
    mine_sent(0)
    mine_sent(1)
    mine_sent(2)
    mine_sent(3)
    line_sent(0)
    line_sent(1)
    line_sent(2)
    line_sent(3)
    ring_sent(0)
    ring_sent(1)
    ring_sent(2)
    ring_sent(3)
    for c in range(CHUNKS):
        arrived(sums_out.at[c], sums_send.at[c])
    for c in range(CHUNKS):
        arrived(sums_in.at[c], sums_recv.at[c])
        for g in range(LINE - 1):
            own[c] = own[c] + sums_in[c, g].astype(jnp.float32)

    low = jnp.concatenate(
        [by_group(half_group, [shift(own[c], c - m) for c in range(CHUNKS)]) for m in range(CHUNKS)], axis=0
    ).astype(jnp.bfloat16)
    mixed = jnp.maximum(jnp.dot(low, weight[...], preferred_element_type=jnp.float32), 0.0).astype(jnp.bfloat16)
    out[...] = jnp.dot(moves[...], mixed, preferred_element_type=jnp.float32).astype(jnp.bfloat16)


def on_device(features, weight, tile_values, tile_rows, tile_cols, tile_count, node_order):
    dma = pltpu.SemaphoreType.DMA
    others = len(OTHERS)
    low = jnp.bfloat16
    operands = (features.reshape(2, TILE, TILE), weight, tile_values, tile_rows, tile_cols, tile_count, node_order)
    return pl.pallas_call(
        kernel,
        out_shape=pltpu.VMEM(features.shape, features.dtype),
        in_specs=[pl.BlockSpec(memory_space=pltpu.HBM)] * 7,
        out_specs=pl.BlockSpec(memory_space=pltpu.VMEM),
        scratch_shapes=[
            pltpu.VMEM((2, TILE, TILE), low),
            pltpu.VMEM(weight.shape, low),
            pltpu.VMEM((SLOTS, TILE, TILE), low),
            pltpu.SMEM(tile_rows.shape, jnp.int32),
            pltpu.SMEM(tile_cols.shape, jnp.int32),
            pltpu.SMEM(tile_count.shape, jnp.int32),
            pltpu.VMEM(node_order.shape, jnp.int32),
            *[pltpu.VMEM((CELLS, HALF, TILE), low)] * CHUNKS,
            pltpu.VMEM((CHUNKS, SLOTS + 1, TILE, TILE), low),
            pltpu.VMEM((2, TILE, 2 * TILE), low),
            pltpu.VMEM((2 * TILE, 2 * TILE), low),
            pltpu.VMEM((CHUNKS, others, TILE + FLAG_ROWS, TILE), low),
            pltpu.VMEM((CHUNKS, others, TILE + FLAG_ROWS, TILE), low),
            pltpu.VMEM((CHUNKS, LINE - 1, HALF, TILE), low),
            pltpu.VMEM((CHUNKS, LINE - 1, HALF, TILE), low),
            dma((7,)),
            dma((CHUNKS, 2)),
            dma((CHUNKS, 2)),
            dma((CHUNKS,)),
            dma((CHUNKS,)),
            dma((CHUNKS,)),
            dma((CHUNKS,)),
            pltpu.SemaphoreType.REGULAR,
        ],
        compiler_params=pltpu.CompilerParams(
            collective_id=0, has_side_effects=True, vmem_limit_bytes=32 * 2**20
        ),
        name="graph_convolution",
    )(
        *(operand if operand is tile_count else pltpu.with_memory_space_constraint(operand, pltpu.HBM) for operand in operands)
    )


def solution(mesh):
    return jax.shard_map(
        on_device,
        mesh=mesh,
        in_specs=(
            P(("col", "row"), None),
            P(),
            P("row", "col", None, None, None),
            P("row", "col", None),
            P("row", "col", None),
            P("row", "col"),
            P(("row", "col")),
        ),
        out_specs=P(("row", "col"), None),
        check_vma=False,
    )
```

time: 48.7 us -> 48.5 us (level)
  the two profiles are of different devices: /device:TPU:32 before, /device:TPU:1 now
where the time goes in v5:
time: 48.5 us; the launch traced here: 48.1 us
  Pallas kernels  46.8 us (96%)
  between operations  0.66 us (1%)
  local copies, waits for them, and re-layouts  0.63 us (1%)
    pallas_call x1, Pallas kernels, on_device(): pl.pallas_call(kernel, out_shape=pltpu.VMEM(features.shape, features.dtyp...  46.8 us

profile of v5, /device:TPU:1, one launch (start us, length us, event | category | flops | bytes accessed | tf_op | source)
XLA Modules:
  0.0 48.1 jit_solution(9343113036184918948)
XLA Ops:
  0.7 46.8 %graph_convolution.1 = bf16[256,128]{1,0:T(8,128)(2,1)S(1)} custom-call(bf16[2,128,128]{2,1,0:T(8,128)(2,1)} %bitcast.1, bf16[128,128]{1,0:T(8,128)(2,1)} %weight_hbm.1, bf16[1,1,16,128,128]{4,3,2,1,0:T(8,128)(2,1)} %tile_values_hbm.1, s32[1,1,16]{2,1,0:T(1,128)} %tile_rows_hbm.1, s32[1,1,16]{2,1,0:T(1,128)} %tile_cols_hbm.1, ...), custom_call_target="tpu_custom_call" | custom-call | tf_op jit(solution)/shard_map/graph_convolution/pallas_call | solution.py:281
  47.5 0.6 %copy.9 = bf16[256,128]{1,0:T(8,128)(2,1)} copy(bf16[256,128]{1,0:T(8,128)(2,1)S(1)} %graph_convolution.1) | data formatting | bytes 131072

commit v6 on v5

--- a/solution.py
+++ b/solution.py
@@ -132,7 +132,7 @@
 
     def send_mine(c):
         mine = gathered[c].at[slot_of(c, row)]
-        for d in (2, 1, 3) if c == LAST else (1, 3, 2):
+        for d in (2, 1, 3):
             to = in_row(z, (x + d) % LINE) if c == LAST else in_row((z + d) % LINE, x)
             send(mine, mine, gather_send.at[c, 0], gather_recv.at[c, 0], to)
 

time: 48.5 us -> 48.4 us (level)
  no operation moved by 1% of the time
where the time goes in v6:
time: 48.4 us; the launch traced here: 48.3 us
  Pallas kernels  47 us (97%)
  between operations  0.66 us (1%)
  local copies, waits for them, and re-layouts  0.63 us (1%)
    pallas_call x1, Pallas kernels, on_device(): pl.pallas_call(kernel, out_shape=pltpu.VMEM(features.shape, features.dtyp...  47 us

profile of v6, /device:TPU:1, one launch (start us, length us, event | category | flops | bytes accessed | tf_op | source)
XLA Modules:
  0.0 48.3 jit_solution(6170569839437557643)
XLA Ops:
  0.7 47.0 %graph_convolution.1 = bf16[256,128]{1,0:T(8,128)(2,1)S(1)} custom-call(bf16[2,128,128]{2,1,0:T(8,128)(2,1)} %bitcast.1, bf16[128,128]{1,0:T(8,128)(2,1)} %weight_hbm.1, bf16[1,1,16,128,128]{4,3,2,1,0:T(8,128)(2,1)} %tile_values_hbm.1, s32[1,1,16]{2,1,0:T(1,128)} %tile_rows_hbm.1, s32[1,1,16]{2,1,0:T(1,128)} %tile_cols_hbm.1, ...), custom_call_target="tpu_custom_call" | custom-call | tf_op jit(solution)/shard_map/graph_convolution/pallas_call | solution.py:281
  47.6 0.6 %copy.9 = bf16[256,128]{1,0:T(8,128)(2,1)} copy(bf16[256,128]{1,0:T(8,128)(2,1)S(1)} %graph_convolution.1) | data formatting | bytes 131072
